TPU v7x, 32 devices: a whole 2x2x4 slice. The times are simulated.
32 devices in a mesh: lag: 4 (over y, x), row: 8 (over z, core).
Axes of the slice: x: 2, y: 2, z: 4, core: 2. Of those that a mesh axis runs over, the one named last changes fastest.
Arguments:
- newest: bfloat16 [512, 8192], P('lag', 'row'), may hold values from -6 to 6
- earlier: bfloat16 [3, 8192], P(None, 'row'), may hold values from -6 to 6
- lag_matrices: bfloat16 [4, 8192, 8192], P('lag', 'row'), may hold values from -0.03125 to 0.03125
Outputs:
- forces: float32 [512, 8192], P('lag', 'row')
All inputs are finite; a program needn't handle non-finite values.
Results may differ from a plain program's by a relative error of at most 0.0003.
Values may be sent and summed in bfloat16 or wider, within the bound.
A program may use at most 64 MiB of HBM per device.

v0:
```python
import jax
import jax.numpy as jnp
from jax import lax
from jax.sharding import PartitionSpec as P


def product(window, matrix):
    return lax.dot_general(
        window, matrix, (((1,), (1,)), ((), ())), preferred_element_type=jnp.float32
    )


def on_device(newest, earlier, lag_matrices):
    lag_index = lax.axis_index("lag")
    matrix = lag_matrices[0]
    own_steps = newest.shape[0]
    earlier_rows = earlier.shape[0]
    wide_newest, wide_earlier = (
        lax.all_gather(newest, "row", axis=1, tiled=True),
        lax.all_gather(earlier, "row", axis=1, tiled=True),
    )
    history = lax.all_gather(wide_newest, "lag", axis=0, tiled=True)
    record = jnp.concatenate([wide_earlier, history], axis=0)
    window = lax.dynamic_slice_in_dim(
        record, jnp.int32(0) + earlier_rows - lag_index, own_steps * lax.axis_size("lag"), 0
    )
    return lax.psum_scatter(product(window, matrix), "lag", scatter_dimension=0, tiled=True)


def solution(mesh):
    in_specs = (P("lag", "row"), P(None, "row"), P("lag", "row", None))
    out_specs = P("lag", "row")
    return jax.shard_map(
        on_device, mesh=mesh, in_specs=in_specs, out_specs=out_specs, check_vma=False
    )
```

profile of v0, /device:TPU:0, one launch (start us, length us, event | category | flops | bytes accessed | tf_op | source)
XLA Modules:
  0.0 187.6 jit_solution(14808230118894259907)
XLA Ops:
  6.5 0.0 all-gather.3.cloned.1.call-start
  6.5 0.7 all-gather.3.cloned.1.call-update
  7.3 0.0 all-gather.5.cloned.1.call-start
  7.3 33.5 %all-gather.3.cloned.1.call-done = bf16[128,8192]{1,0:T(8,128)(2,1)} async-done(((bf16[128,1024]{1,0:T(8,128)(2,1)}), bf16[128,8192]{1,0:T(8,128)(2,1)}) %all-gather.3.cloned.1.call-update) | async-done | bytes 2097168 | tf_op jit(solution)/shard_map/all_gather | solution.py:19
  40.8 0.0 all-gather.5.cloned.1.call-update
  40.8 0.0 reduce-scatter.2.cloned.1.call-start
  40.9 14.2 %all_gather.9 = bf16[3,8192]{1,0:T(4,128)(2,1)S(1)} all-gather(bf16[3,1024]{1,0:T(4,128)(2,1)} %param.4), channel_id=1, replica_groups=mesh['lag'=4,'row'=8] {'row'}, dimensions={1}, use_global_device_ids=true | all-gather | bytes 55296 | tf_op jit(solution)/shard_map/all_gather | solution.py:20
  55.1 74.7 %all-gather.5.cloned.1.call-done = bf16[512,8192]{1,0:T(8,128)(2,1)} async-done(((bf16[128,8192]{1,0:T(8,128)(2,1)}), bf16[512,8192]{1,0:T(8,128)(2,1)}) %all-gather.5.cloned.1.call-update) | async-done | bytes 8388624 | tf_op jit(solution)/shard_map/all_gather | solution.py:22
  129.8 15.9 %fusion = f32[512,1024]{1,0:T(8,128)} fusion(bf16[1,1024,8192]{2,1,0:T(8,128)(2,1)} %param.5, s32[]{:T(128)S(6)} %select_n.3, bf16[3,8192]{1,0:T(4,128)(2,1)S(1)} %all_gather.9, bf16[512,8192]{1,0:T(8,128)(2,1)} %all-gather.5.cloned.1.call-done), kind=kOutput, calls=%fused_computation | convolution fusion | flops 8606711808 | bytes 27312132 | tf_op jit(solution)/shard_map/dot_general | solution.py:8
  145.6 0.0 reduce-scatter.2.cloned.1.call-update
  145.7 35.4 %reduce-scatter.2.cloned.1.call-done = f32[128,1024]{1,0:T(8,128)} async-done(((f32[512,1024]{1,0:T(8,128)}), f32[128,1024]{1,0:T(8,128)}) %reduce-scatter.2.cloned.1.call-update) | async-done | bytes 524304 | tf_op jit(solution)/shard_map/reduce_scatter | solution.py:27
Async XLA Ops:
  6.5 34.3 %all-gather.3.cloned.1.call-start = ((), (), s32[]{:S(2)}) async-start(), calls=%async_computation.1 | async-start | bytes 2359296 | tf_op jit(solution)/shard_map/all_gather | solution.py:19
  7.3 122.5 %all-gather.5.cloned.1.call-start = ((), (), s32[]{:S(2)}) async-start(), calls=%async_computation.2 | async-start | bytes 10485760 | tf_op jit(solution)/shard_map/all_gather | solution.py:22
  40.8 140.2 %reduce-scatter.2.cloned.1.call-start = ((), (), s32[]{:S(2)}) async-start(), calls=%async_computation.3 | async-start | bytes 2621440 | tf_op jit(solution)/shard_map/reduce_scatter | solution.py:27
Sparse Core Ops, SparseCore 0:
  9.0 31.7 all-gather.2
  42.6 87.0 all-gather.4
  145.8 35.2 reduce-scatter.1
where the time goes:
time: 188 us
  waiting for transfers between devices  144 us (77%)
  matrix products  15.9 us (8%)
  blocking collectives  14.2 us (8%)
  between operations  13.1 us (7%)
    all_gather x1, waiting for transfers between devices, on_device(): history = lax.all_gather(wide_newest, 'lag', axis=0, tiled=True)  74.7 us
    reduce_scatter x1, waiting for transfers between devices, on_device(): lax.psum_scatter(product(window, matrix), 'lag', scatter_dimension=0, til...  35.4 us
    all_gather x1, waiting for transfers between devices, on_device(): lax.all_gather(newest, 'row', axis=1, tiled=True)  33.5 us
    dot_general x1, matrix products, product(): lax.dot_general(window, matrix, (((1,), (1,)), ((), ())), preferred_eleme...  15.9 us
    all_gather x1, blocking collectives, on_device(): lax.all_gather(earlier, 'row', axis=1, tiled=True)  14.2 us
  transfers between devices with their start and end apart: 3, of which 3 were waited for; matrix products, arithmetic and copies ran while one was open for 0% of the time, Pallas kernels for 0%

commit v1 on v0

v1 whole, which is shorter than its diff:
```python
import jax
import jax.numpy as jnp
from jax import lax
from jax.experimental import pallas as pl
from jax.experimental.pallas import tpu as pltpu
from jax.sharding import PartitionSpec as P

MESH = pl.DeviceIdType.MESH
PAD = 16
NZ = 4


def product(window, matrix):
    return lax.dot_general(
        window, matrix, (((1,), (1,)), ((), ())), preferred_element_type=jnp.float32
    )


def on_device_general(newest, earlier, lag_matrices):
    lag_index = lax.axis_index("lag")
    matrix = lag_matrices[0]
    own_steps = newest.shape[0]
    earlier_rows = earlier.shape[0]
    wide_newest, wide_earlier = (
        lax.all_gather(newest, "row", axis=1, tiled=True),
        lax.all_gather(earlier, "row", axis=1, tiled=True),
    )
    history = lax.all_gather(wide_newest, "lag", axis=0, tiled=True)
    record = jnp.concatenate([wide_earlier, history], axis=0)
    window = lax.dynamic_slice_in_dim(
        record, jnp.int32(0) + earlier_rows - lag_index, own_steps * lax.axis_size("lag"), 0
    )
    return lax.psum_scatter(product(window, matrix), "lag", scatter_dimension=0, tiled=True)


def kernel(new_ref, ear_ref, mat_ref, out_ref,
           mat, hist, ebuf, acc, s_d, s_x, s_y, r_d, r_1, r_2,
           loc, zs, zr, xs, xr, ys, yr, ss, sr, es, er, fs, fr):
    lag, row = lax.axis_index("lag"), lax.axis_index("row")
    x, y = lag % 2, lag // 2
    z, core = row // 2, row % 2
    sib = row + 1 - 2 * core
    t0, tx, ty = lag, 2 * y + 1 - x, 2 * (1 - y) + x
    td = 2 * (1 - y) + 1 - x
    steps, width = new_ref.shape
    half = steps // 2
    x_dev, y_dev = {"lag": tx, "row": row}, {"lag": ty, "row": row}
    sib_dev = {"lag": lag, "row": sib}

    mat_copy = pltpu.make_async_copy(mat_ref.at[0], mat, loc.at[0])
    mat_copy.start()

    def rows(t, h, n):
        return pl.ds(pl.multiple_of(PAD + t * steps + h * half, 16), n)

    own_copy = pltpu.make_async_copy(new_ref, hist.at[row, rows(t0, 0, steps)], loc.at[1])
    own_copy.start()
    own_e = pltpu.make_async_copy(ear_ref, ebuf.at[row], loc.at[2])
    own_e.start()

    barrier = pltpu.get_barrier_semaphore()
    for dev in (x_dev, y_dev):
        pl.semaphore_signal(barrier, inc=1, device_id=dev, device_id_type=MESH)
    for j in range(1, 2 * NZ):
        pl.semaphore_signal(barrier, inc=1, device_id={"lag": lag, "row": (row + j) % (2 * NZ)},
                            device_id_type=MESH)
    pl.semaphore_wait(barrier, 2 * NZ + 1)

    def copy(src, dst, ssem, rsem, dev):
        return pltpu.make_async_remote_copy(
            src_ref=src, dst_ref=dst, send_sem=ssem, recv_sem=rsem, device_id=dev,
            device_id_type=MESH)

    def place(r, t, h, n):
        return hist.at[r, rows(t, h, n)]

    z_kind = ((t0, 0, steps), (tx, 0, half), (ty, 1, half))
    x_kind = ((t0, 0, half), (t0, 1, half), (ty, 1, half))
    y_kind = ((t0, 1, half), (t0, 0, half), (tx, 0, half))
    s_kind = tuple((t, 0, steps) for t in (t0, tx, ty, td))
    x_got = ((tx, 0, half), (tx, 1, half), (td, 1, half))
    y_got = ((ty, 1, half), (ty, 0, half), (td, 0, half))

    def fam(zz):
        return 2 * zz + core

    def z_msg(up, zz, m):
        dev = {"lag": lag, "row": row + 2 if up else row - 2}
        ref = place(fam(zz), *z_kind[m])
        return copy(ref, ref, zs.at[int(up), zz, m], zr.at[zz, m], dev)

    def z_own(up):
        dev = {"lag": lag, "row": row + 2 if up else row - 2}
        return copy(new_ref, place(row, *z_kind[0]), zs.at[int(up), z, 0], zr.at[z, 0], dev)

    def x_msg(zz, m):
        ref = place(fam(zz), *x_kind[m])
        return copy(ref, ref, xs.at[zz, m], xr.at[zz, m], x_dev)

    def y_msg(zz, m):
        ref = place(fam(zz), *y_kind[m])
        return copy(ref, ref, ys.at[zz, m], yr.at[zz, m], y_dev)

    def s_msg(zz, m):
        ref = place(fam(zz), *s_kind[m])
        return copy(ref, ref, ss.at[zz, m], sr.at[zz, m], sib_dev)

    def z_wait(zz, m):
        ref = place(fam(zz), *z_kind[m])
        copy(ref, ref, zs.at[0, zz, m], zr.at[zz, m], x_dev).wait_recv()

    def x_wait(zz, m):
        ref = place(fam(zz), *x_got[m])
        copy(ref, ref, xs.at[zz, m], xr.at[zz, m], x_dev).wait_recv()

    def y_wait(zz, m):
        ref = place(fam(zz), *y_got[m])
        copy(ref, ref, ys.at[zz, m], yr.at[zz, m], y_dev).wait_recv()

    def s_wait(zz, m):
        ref = place(2 * zz + 1 - core, *s_kind[m])
        copy(ref, ref, ss.at[zz, m], sr.at[zz, m], sib_dev).wait_recv()

    can_up, can_down = z < NZ - 1, z > 0

    def own_half(h):
        return new_ref.at[pl.ds(h * half, half)]

    @pl.when(can_up)
    def _():
        z_own(True).start()

    @pl.when(can_down)
    def _():
        z_own(False).start()

    own_x = [copy(own_half(h), place(row, t0, h, half), xs.at[z, h], xr.at[z, h], x_dev)
             for h in (0, 1)]
    own_y = [copy(own_half(1 - m), place(row, t0, 1 - m, half), ys.at[z, m], yr.at[z, m], y_dev)
             for m in (0, 1)]
    for m in (0, 1):
        own_x[m].start()
        own_y[m].start()
    copy(new_ref, place(row, t0, 0, steps), ss.at[z, 0], sr.at[z, 0], sib_dev).start()

    def e_msg(j):
        to = (row + j) % (2 * NZ)
        return copy(ear_ref, ebuf.at[row], es.at[j], er.at[row], {"lag": lag, "row": to})

    def e_wait(j):
        frm = (row + j) % (2 * NZ)
        copy(ear_ref, ebuf.at[frm], es.at[j], er.at[frm], sib_dev).wait_recv()

    for j in range(1, 2 * NZ):
        e_msg(j).start()

    def z_on_both(m):
        @pl.when(can_up)
        def _():
            z_msg(True, z, m).start()

        @pl.when(can_down)
        def _():
            z_msg(False, z, m).start()

    def arrive(zz, m, up):
        z_wait(zz, m)

        @pl.when(can_up if up else can_down)
        def _():
            z_msg(up, zz, m).start()

        if m == 0:
            x_msg(zz, 1).start()
            y_msg(zz, 1).start()
            s_msg(zz, 0).start()
        elif m == 1:
            y_msg(zz, 2).start()
        else:
            x_msg(zz, 2).start()

    def both(d, act):
        @pl.when(z >= d)
        def _():
            act(z - d, True)

        @pl.when(z + d < NZ)
        def _():
            act(z + d, False)

    def rest(zz):
        x_wait(zz, 1)
        s_msg(zz, 1).start()
        y_wait(zz, 1)
        s_msg(zz, 2).start()
        x_wait(zz, 2)
        y_wait(zz, 2)
        s_msg(zz, 3).start()

    tile = 256

    def compute(zz, first=False):
        for m in range(4):
            s_wait(zz, m)

        def body(i, carry):
            n = pl.ds(pl.multiple_of(i * tile, tile), tile)
            total = None
            for c in range(2):
                r = 2 * zz + c
                cols = pl.ds(pl.multiple_of(r * width, width), width)
                term = product(hist[r], mat[n, cols])
                total = term if total is None else total + term
            if first:
                acc[:, n] = total
            else:
                acc[:, n] += total
            return carry

        lax.fori_loop(0, acc.shape[1] // tile, body, 0)

    x_wait(z, 0)
    z_on_both(1)
    y_msg(z, 2).start()
    y_wait(z, 0)
    z_on_both(2)
    x_msg(z, 2).start()
    both(1, lambda zz, up: arrive(zz, 0, up))
    own_copy.wait()
    own_e.wait()
    rest(z)
    for m in (1, 2):
        both(1, lambda zz, up: arrive(zz, m, up))
    for j in range(1, 2 * NZ):
        e_wait(j)
    chunk = ear_ref.shape[1]
    for r in range(2 * NZ):
        e = ebuf[r].astype(jnp.float32)
        for j in range(width // chunk):
            cut = 4 * j + 4
            piece = e if cut == PAD else jnp.concatenate([e[cut:], e[:cut]], axis=0)
            hist[r, 0:PAD, j * chunk:(j + 1) * chunk] = piece.astype(hist.dtype)
    mat_copy.wait()
    compute(z, first=True)
    for d in (2, 3):
        both(d, lambda zz, up: arrive(zz, 0, up))
        both(d - 1, lambda zz, up: rest(zz))
        if d == 2:
            for m in (1, 2):
                both(d, lambda zz, up: arrive(zz, m, up))
            both(1, lambda zz, up: compute(zz))
        else:
            for m in (1, 2):
                both(d, lambda zz, up: arrive(zz, m, up))
            both(2, lambda zz, up: compute(zz))
    both(3, lambda zz, up: rest(zz))
    both(3, lambda zz, up: compute(zz))

    def shifted(t, h, n0):
        start = pl.multiple_of(PAD - 8 + t * steps + h * half, 8)
        part = acc[pl.ds(start, half + 8), n0:n0 + tile]
        got = part[8:]
        for k in range(1, 4):
            got = jnp.where(lag == k, part[8 - k:8 - k + half], got)
        return got

    def fill(dst, t, h):
        for n0 in range(0, width, tile):
            dst[h * half:(h + 1) * half, n0:n0 + tile] = shifted(t, h, n0)

    def f_msg(src, dst, h, i, dev):
        cut = pl.ds(h * half, half)
        return copy(src.at[cut], dst.at[cut], fs.at[i], fr.at[i], dev)

    hop_y, hop_x = f_msg(s_d, r_d, 0, 0, y_dev), f_msg(s_d, r_d, 1, 1, x_dev)
    dir_x, dir_y = f_msg(s_x, r_1, 1, 2, x_dev), f_msg(s_y, r_1, 0, 3, y_dev)
    last_x, last_y = f_msg(s_x, r_2, 0, 4, x_dev), f_msg(s_y, r_2, 1, 5, y_dev)
    fill(s_d, td, 0)
    hop_y.start()
    fill(s_d, td, 1)
    hop_x.start()
    fill(s_x, tx, 1)
    dir_x.start()
    fill(s_y, ty, 0)
    dir_y.start()
    fill(s_x, tx, 0)
    fill(s_y, ty, 1)
    hop_y.wait_recv()
    s_x[0:half] += r_d[0:half]
    last_x.start()
    hop_x.wait_recv()
    s_y[half:steps] += r_d[half:steps]
    last_y.start()
    fill(out_ref, t0, 0)
    fill(out_ref, t0, 1)
    dir_x.wait_recv()
    dir_y.wait_recv()
    out_ref[...] += r_1[...]
    last_x.wait_recv()
    out_ref[0:half] += r_2[0:half]
    last_y.wait_recv()
    out_ref[half:steps] += r_2[half:steps]

    for c in (hop_y, hop_x, dir_x, dir_y, last_x, last_y):
        c.wait_send()
    for j in range(1, 2 * NZ):
        e_msg(j).wait_send()
    x_msg(z, 0).wait_send()
    y_msg(z, 0).wait_send()
    for zz in range(NZ):
        for m in range(3):
            @pl.when(can_up & (z >= zz))
            def _():
                z_msg(True, zz, m).wait_send()

            @pl.when(can_down & (z <= zz))
            def _():
                z_msg(False, zz, m).wait_send()
        for m in (1, 2):
            x_msg(zz, m).wait_send()
            y_msg(zz, m).wait_send()
        for m in range(4):
            s_msg(zz, m).wait_send()


def on_device(newest, earlier, lag_matrices):
    steps, width = newest.shape
    height = lag_matrices.shape[1]
    count = earlier.shape[0]
    groups = PAD // 4
    packed = jnp.pad(earlier, ((4 - count, 0), (0, 0)))
    packed = packed.reshape(4, groups, width // groups).transpose(1, 0, 2).reshape(PAD, width // groups)
    any_spec = pl.BlockSpec(memory_space=pl.ANY)
    vmem = pl.BlockSpec(memory_space=pltpu.VMEM)
    dma = pltpu.SemaphoreType.DMA
    block = pltpu.VMEM((steps, height), jnp.float32)
    return pl.pallas_call(
        kernel,
        out_shape=jax.ShapeDtypeStruct((steps, height), jnp.float32),
        in_specs=[any_spec, any_spec, any_spec],
        out_specs=vmem,
        scratch_shapes=[
            pltpu.VMEM((height, 2 * NZ * width), jnp.bfloat16),
            pltpu.VMEM((2 * NZ, PAD + 4 * steps, width), jnp.bfloat16),
            pltpu.VMEM((2 * NZ, PAD, width // groups), jnp.bfloat16),
            pltpu.VMEM((PAD + 4 * steps, height), jnp.float32),
            block, block, block, block, block, block,
            dma((3,)),
            dma((2, NZ, 3)), dma((NZ, 3)),
            dma((NZ, 3)), dma((NZ, 3)),
            dma((NZ, 3)), dma((NZ, 3)),
            dma((NZ, 4)), dma((NZ, 4)),
            dma((2 * NZ,)), dma((2 * NZ,)),
            dma((6,)), dma((6,)),
        ],
        compiler_params=pltpu.CompilerParams(
            collective_id=0, has_side_effects=True, vmem_limit_bytes=48 * 1024 * 1024
        ),
        cost_estimate=pl.CostEstimate(
            flops=2 * 4 * steps * height * 2 * NZ * width,
            bytes_accessed=height * 2 * NZ * width * 2, transcendentals=0),
    )(newest, packed, lag_matrices)


def solution(mesh):
    in_specs = (P("lag", "row"), P(None, "row"), P("lag", "row", None))
    out_specs = P("lag", "row")
    fits = mesh.shape["lag"] == 4 and mesh.shape["row"] == 2 * NZ
    return jax.shard_map(
        on_device if fits else on_device_general,
        mesh=mesh, in_specs=in_specs, out_specs=out_specs, check_vma=False
    )
```

time: 188 us -> 73.1 us (0.39)
  waiting for transfers between devices: 144 us -> 0 us
  Pallas kernels: 0 us -> 70.4 us
  matrix products: 15.9 us -> 0 us
  blocking collectives: 14.2 us -> 0 us
  between operations: 13.1 us -> 0.02 us
  local copies, waits for them, and re-layouts: 0 us -> 2.46 us
    all_gather x2 -> x0, waiting for transfers between devices: 108 us -> none  [the longest x1 74.7 us: on_device(): history = lax.all_gather(wide_newest, 'lag', axis=0, tiled=True)]
    pallas_call x0 -> x1, Pallas kernels: none -> 70.4 us  [on_device(): pl.pallas_call(kernel, out_shape=jax.ShapeDtypeStruct((steps, height), jn...]
    reduce_scatter x1 -> x0, waiting for transfers between devices: 35.4 us -> none  [on_device(): lax.psum_scatter(product(window, matrix), 'lag', scatter_dimension=0, til...]
    dot_general x1 -> x0, matrix products: 15.9 us -> none  [product(): lax.dot_general(window, matrix, (((1,), (1,)), ((), ())), preferred_eleme...]
    all_gather x1 -> x0, blocking collectives: 14.2 us -> none  [on_device(): lax.all_gather(earlier, 'row', axis=1, tiled=True)]
  transfers between devices with their start and end apart: 3 -> 0, of which waited for: 3 -> 0; matrix products, arithmetic and copies ran while one was open for 0% -> 0% of each run, Pallas kernels for 0% -> 0%
where the time goes in v1:
time: 73.1 us; the launch traced here: 72.9 us
  Pallas kernels  70.4 us (96%)
  local copies, waits for them, and re-layouts  2.46 us (3%)
    pallas_call x1, Pallas kernels, on_device(): pl.pallas_call(kernel, out_shape=jax.ShapeDtypeStruct((steps, height), jn...  70.4 us
    unnamed x3, local copies, waits for them, and re-layouts  1.74 us

profile of v1, /device:TPU:0, one launch (start us, length us, event | category | flops | bytes accessed | tf_op | source)
XLA Modules:
  0.0 72.9 jit_solution(9904376793229185210)
XLA Ops:
  0.0 0.7 pad.4
  0.7 0.0 copy-start
  0.7 0.9 %copy-done = bf16[128,1024]{1,0:T(8,128)(2,1)S(1)} copy-done((bf16[128,1024]{1,0:T(8,128)(2,1)S(1)}, bf16[128,1024]{1,0:T(8,128)(2,1)}, u32[]{:S(2)}) %copy-start) | copy-done | bytes 262168
  1.7 70.4 %shard_map.37 = f32[128,1024]{1,0:T(8,128)S(1)} custom-call(bf16[128,1024]{1,0:T(8,128)(2,1)S(1)} %copy-done, bf16[16,256]{1,0:T(8,128)(2,1)S(1)} %reshape.7.ear_ref, bf16[1,1024,8192]{2,1,0:T(8,128)(2,1)} %mat_ref.1), custom_call_target="tpu_custom_call" | custom-call | flops 8589934592 | bytes 16777216 | tf_op jit(solution)/shard_map/pallas_call | solution.py:337
  72.1 0.8 %copy.6 = f32[128,1024]{1,0:T(8,128)} copy(f32[128,1024]{1,0:T(8,128)S(1)} %shard_map.37) | data formatting | bytes 1048576
  (1 shorter events, 0.0 us)
Async XLA Ops:
  0.7 1.0 %copy-start = (bf16[128,1024]{1,0:T(8,128)(2,1)S(1)}, bf16[128,1024]{1,0:T(8,128)(2,1)}, u32[]{:S(2)}) copy-start(bf16[128,1024]{1,0:T(8,128)(2,1)} %new_ref.1) | copy-start | bytes 786436

commit v2 on v1

--- a/solution.py
+++ b/solution.py
@@ -154,12 +154,15 @@
     for j in range(1, 2 * NZ):
         e_msg(j).start()
 
+    wide_up, wide_down = z < NZ - 2, z > 1
+    at_end = (z == 0) | (z == NZ - 1)
+
     def z_on_both(m):
-        @pl.when(can_up)
+        @pl.when(wide_up)
         def _():
             z_msg(True, z, m).start()
 
-        @pl.when(can_down)
+        @pl.when(wide_down)
         def _():
             z_msg(False, z, m).start()
 
@@ -197,7 +200,7 @@
         y_wait(zz, 2)
         s_msg(zz, 3).start()
 
-    tile = 256
+    tile = 512
 
     def compute(zz, first=False):
         for m in range(4):
@@ -225,12 +228,37 @@
     y_wait(z, 0)
     z_on_both(2)
     x_msg(z, 2).start()
-    both(1, lambda zz, up: arrive(zz, 0, up))
+    inner = jnp.where(z == 0, 1, NZ - 2)
+
+    @pl.when(at_end)
+    def _():
+        z_wait(inner, 0)
+        for m in (0, 1):
+            x_msg(inner, m).start()
+            y_msg(inner, m).start()
+        s_msg(inner, 0).start()
+
+    @pl.when(jnp.logical_not(at_end))
+    def _():
+        arrive(z - 1, 0, True)
+        arrive(z + 1, 0, False)
+
     own_copy.wait()
     own_e.wait()
     rest(z)
-    for m in (1, 2):
-        both(1, lambda zz, up: arrive(zz, m, up))
+    @pl.when(at_end)
+    def _():
+        x_wait(inner, 0)
+        y_msg(inner, 2).start()
+        y_wait(inner, 0)
+        x_msg(inner, 2).start()
+
+    @pl.when(jnp.logical_not(at_end))
+    def _():
+        for m in (1, 2):
+            arrive(z - 1, m, True)
+            arrive(z + 1, m, False)
+
     for j in range(1, 2 * NZ):
         e_wait(j)
     chunk = ear_ref.shape[1]
@@ -258,15 +286,15 @@
 
     def shifted(t, h, n0):
         start = pl.multiple_of(PAD - 8 + t * steps + h * half, 8)
-        part = acc[pl.ds(start, half + 8), n0:n0 + tile]
+        part = acc[pl.ds(start, half + 8), n0:n0 + 256]
         got = part[8:]
         for k in range(1, 4):
             got = jnp.where(lag == k, part[8 - k:8 - k + half], got)
         return got
 
     def fill(dst, t, h):
-        for n0 in range(0, width, tile):
-            dst[h * half:(h + 1) * half, n0:n0 + tile] = shifted(t, h, n0)
+        for n0 in range(0, width, 256):
+            dst[h * half:(h + 1) * half, n0:n0 + 256] = shifted(t, h, n0)
 
     def f_msg(src, dst, h, i, dev):
         cut = pl.ds(h * half, half)
@@ -307,13 +335,19 @@
         e_msg(j).wait_send()
     x_msg(z, 0).wait_send()
     y_msg(z, 0).wait_send()
+
+    @pl.when(at_end)
+    def _():
+        x_msg(inner, 0).wait_send()
+        y_msg(inner, 0).wait_send()
+
     for zz in range(NZ):
         for m in range(3):
-            @pl.when(can_up & (z >= zz))
+            @pl.when(can_up & (z >= zz) & ((z != zz) | wide_up | (m == 0)))
             def _():
                 z_msg(True, zz, m).wait_send()
 
-            @pl.when(can_down & (z <= zz))
+            @pl.when(can_down & (z <= zz) & ((z != zz) | wide_down | (m == 0)))
             def _():
                 z_msg(False, zz, m).wait_send()
         for m in (1, 2):

time: 73.1 us -> 67.8 us (0.927)
  Pallas kernels: 70.4 us -> 65 us
    pallas_call x1, Pallas kernels: 70.4 us -> 65 us  [on_device(): pl.pallas_call(kernel, out_shape=jax.ShapeDtypeStruct((steps, height), jn...]
where the time goes in v2:
time: 67.8 us; the launch traced here: 67.5 us
  Pallas kernels  65 us (96%)
  local copies, waits for them, and re-layouts  2.46 us (4%)
    pallas_call x1, Pallas kernels, on_device(): pl.pallas_call(kernel, out_shape=jax.ShapeDtypeStruct((steps, height), jn...  65 us
    unnamed x3, local copies, waits for them, and re-layouts  1.74 us

profile of v2, /device:TPU:0, one launch (start us, length us, event | category | flops | bytes accessed | tf_op | source)
XLA Modules:
  0.0 67.5 jit_solution(98821681164382991)
XLA Ops:
  0.0 0.7 %pad.4 = bf16[4,1024]{1,0:T(4,128)(2,1)S(1)} pad(bf16[3,1024]{1,0:T(4,128)(2,1)} %param.4, bf16[]{:T(256)} %constant.2.clone.1), padding=1_0x0_0 | pad | bytes 14338 | tf_op jit(solution)/shard_map/jit(_pad)/pad | solution.py:365
  0.7 0.0 copy-start
  0.7 0.9 %copy-done = bf16[128,1024]{1,0:T(8,128)(2,1)S(1)} copy-done((bf16[128,1024]{1,0:T(8,128)(2,1)S(1)}, bf16[128,1024]{1,0:T(8,128)(2,1)}, u32[]{:S(2)}) %copy-start) | copy-done | bytes 262168
  1.7 65.0 %shard_map.37 = f32[128,1024]{1,0:T(8,128)S(1)} custom-call(bf16[128,1024]{1,0:T(8,128)(2,1)S(1)} %copy-done, bf16[16,256]{1,0:T(8,128)(2,1)S(1)} %reshape.7.ear_ref, bf16[1,1024,8192]{2,1,0:T(8,128)(2,1)} %mat_ref.1), custom_call_target="tpu_custom_call" | custom-call | flops 8589934592 | bytes 16777216 | tf_op jit(solution)/shard_map/pallas_call | solution.py:371
  66.7 0.8 %copy.6 = f32[128,1024]{1,0:T(8,128)} copy(f32[128,1024]{1,0:T(8,128)S(1)} %shard_map.37) | data formatting | bytes 1048576
  (1 shorter events, 0.0 us)
Async XLA Ops:
  0.7 1.0 %copy-start = (bf16[128,1024]{1,0:T(8,128)(2,1)S(1)}, bf16[128,1024]{1,0:T(8,128)(2,1)}, u32[]{:S(2)}) copy-start(bf16[128,1024]{1,0:T(8,128)(2,1)} %new_ref.1) | copy-start | bytes 786436
